TPU v7x, 128 devices: a whole 4x4x4 slice. The times are simulated.
128 devices in a mesh: dp: 8 (over y, core), tm: 16 (over z, x).
Axes of the slice: x: 4, y: 4, z: 4, core: 2. Of those that a mesh axis runs over, the one named last changes fastest.
Arguments:
- signal: bfloat16 [8, 256, 32768], P('dp', None, 'tm'), may hold values from -6 to 6
- lengths: int32 [8, 5], P('dp'), may hold values from 1 to 256, 512 in all within a row
- conv_dilated: bfloat16 [2, 256, 1792], replicated, may hold values from -0.125 to 0.125
- conv_point: bfloat16 [2, 256, 256], replicated, may hold values from -0.375 to 0.375
- conv_down: bfloat16 [16, 512, 256], replicated, may hold values from -0.09375 to 0.09375
- snake_alpha: float32 [5, 256], replicated, may hold values from 0.3 to 3
- out_grad: bfloat16 [8, 512, 4096], P('dp', None, 'tm'), may hold values from -6 to 6
Outputs:
- block_output: bfloat16 [8, 512, 4096], P('dp', None, 'tm')
- signal_grad: bfloat16 [8, 256, 32768], P('dp', None, 'tm')
- grad_dilated: float32 [2, 256, 1792], replicated
- grad_point: float32 [2, 256, 256], replicated
- grad_down: float32 [16, 512, 256], replicated
- grad_alpha: float32 [5, 256], replicated
Inputs may be any that keep to these rules, and one draw needn't show every extreme that they name: Each row packs 4 recordings end to end from the group's first sample, their lengths in tiles of 64 samples, followed by the number of unused tiles at the group's end; a row sums to 512 and its largest entry is exactly 256.
All inputs are finite; a program needn't handle non-finite values.
Results may differ from a plain program's by a relative error of at most 0.038.
The roundings to bfloat16 on the way count: a program that leaves them out, or rounds other values in their place, can miss the bound.
Values may be sent and summed in bfloat16 or wider, within the bound.
A program may use at most 192 MiB of HBM per device.

v0:
```python
import functools

import jax
import jax.numpy as jnp
from jax import lax
from jax.experimental import pallas as pl
from jax.experimental.pallas import tpu as pltpu
from jax.sharding import PartitionSpec as P

TAPS = 7
STRIDE = 8
DILATIONS = (3, 9)
TILE = 64
REC = 4
C = 256
LEAD = 112
F32 = jnp.float32
BF16 = jnp.bfloat16

SIN_PI = (3.14158202, -5.16714279, 2.54189898, -0.55463609)
TWO_COS_PI = (1.9999999, -9.86958572, 8.11682382, -2.66376026, 0.43939346)


def dot(a, b):
    return jnp.dot(a, b, preferred_element_type=F32)


def dot_nt(a, b):
    return lax.dot_general(a, b, (((1,), (1,)), ((), ())), preferred_element_type=F32)


def poly(coefs, x):
    total = coefs[-1]
    for c in coefs[-2::-1]:
        total = total * x + c
    return total


def sine_parts(turns):
    f = turns - jnp.round(turns)
    x = f * f
    s = f * poly(SIN_PI, x)
    return s * poly(TWO_COS_PI, x), s * s


RING = 4
MESH = pl.DeviceIdType.MESH
ORDERS = ((0, 1, 2), (1, 2, 0), (2, 0, 1), (0, 2, 1), (1, 2, 0), (2, 0, 1), (1, 2, 0), (2, 0, 1))
JOB_ROWS = (2048,) * 4 + (1024,) * 4


class Links:
    def __init__(self):
        self.dp, self.tm = lax.axis_index("dp"), lax.axis_index("tm")
        self.core = lax.rem(self.dp, 2)
        self.place = (lax.rem(self.tm, RING), self.dp // 2, self.tm // RING)
        self.sibling = (self.dp + 1 - 2 * self.core, self.tm)
        self.sends = []

    def along(self, axis, step):
        x, y, z = (
            lax.rem(c + step + RING, RING) if a == axis else c for a, c in enumerate(self.place)
        )
        return (y * 2 + self.core, z * RING + x)

    def in_time(self, step):
        count = lax.axis_size("tm")
        return (self.dp, lax.rem(self.tm + step + count, count))

    def peers(self):
        ring = [self.along(a, s) for a in range(3) for s in (1, 2, 3)]
        return [self.sibling, self.in_time(1), self.in_time(-1)] + ring

    def greet(self):
        barrier = pltpu.get_barrier_semaphore()
        for peer in self.peers():
            pl.semaphore_signal(barrier, inc=1, device_id=peer, device_id_type=MESH)

    def met(self):
        pl.semaphore_wait(pltpu.get_barrier_semaphore(), len(self.peers()))

    def remote(self, src, dst, send_sem, recv_sem, dev):
        return pltpu.make_async_remote_copy(
            src_ref=src, dst_ref=dst, send_sem=send_sem, recv_sem=recv_sem,
            device_id=dev, device_id_type=MESH,
        )

    def send(self, *args):
        copy = self.remote(*args)
        copy.start()
        self.sends.append(copy)

    def drain(self):
        for copy in self.sends:
            copy.wait_send()


def block_kernel(samples, len_ref, sig_ref, og_ref, wd_ref, wp_ref, wdn_hbm, al_ref,
                 out_ref, sg_ref, fdn_ref, fw_ref, fa_ref,
                 cols, af0, af1, df0, df1, u0, u1, a0, b0, b1, grad, slope, sa, tr, zcols,
                 gb, gtf, gt, wt, wpt, rem, kcol, acc, hbuf, wdn_ref, gdn, gw, ga,
                 pr_dn, pr_w, land_dn, land_w, fin, gr, gat,
                 load_sem, halo_s, halo_r, pair_s, pair_r, rs_s, rs_r, ag_s, ag_r, fin_sem, back_s, back_r, ga_s, ga_r):
    load = pltpu.make_async_copy(wdn_hbm, wdn_ref, load_sem)
    load.start()
    links = Links()
    links.greet()
    jobs = []

    def tick():
        for job in list(jobs):
            if next(job, True):
                jobs.remove(job)

    u_of, b_of = (u0, u1), (b0, b1)
    af, df = (af0, af1), (df0, df1)
    rows_all = u0.shape[0]
    own0, own1 = LEAD, LEAD + samples
    wide = (own0 - 64, own1 + 64)
    near = (own0 - 32, own1 + 32)
    own_rows = (own0, own1)
    rows_j = samples // STRIDE
    all_j = rows_j + 16
    anchor = lax.axis_index("tm") * samples
    halves = (slice(0, 128), slice(128, 256))

    core = links.core
    place = links.place

    def job_rows(p, hf):
        if p < 4:
            return gdn, fdn_ref, hf * 4 * JOB_ROWS[0] + p * JOB_ROWS[0]
        unit, sub = (p - 4) // 2, (p - 4) % 2
        return gw, fw_ref, (unit * 4 + hf * 2 + sub) * JOB_ROWS[4]

    def at(ref, start, count):
        return ref.at[pl.ds(pl.multiple_of(start, 16), count), :]

    def wrap(c):
        return lax.rem(c + RING, RING)

    def add_rows(dst, d0, terms, count):
        step_rows = min(count, 128)

        def one(i, _):
            v = None
            for ref, r0 in terms:
                t = ref[pl.ds(pl.multiple_of(r0 + i * step_rows, 16), step_rows), :].astype(F32)
                v = t if v is None else v + t
            dst[pl.ds(pl.multiple_of(d0 + i * step_rows, 16), step_rows), :] = v.astype(dst.dtype)
            return 0

        lax.fori_loop(0, count // step_rows, one, 0)

    def job(p):
        axes = ORDERS[p]
        part = JOB_ROWS[p]
        chunk = part // RING
        src, res, other_row = job_rows(p, 1 - core)
        own_row = job_rows(p, core)[2]
        w, land = (pr_dn.at[p], land_dn.at[p]) if p < 4 else (pr_w.at[p - 4], land_w.at[p - 4])
        last = fin.at[p, 0 : part // RING**3, :]
        ring_first = p < 4

        def result(row, count):
            return at(res, own_row + row, count)

        def rs(s, i):
            return rs_s.at[(p * 3 + s) * 4 + i], rs_r.at[(p * 3 + s) * 4 + i]

        def ag(s, i):
            return ag_s.at[(p * 3 + s) * 4 + i], ag_r.at[(p * 3 + s) * 4 + i]

        links.send(at(src, other_row, part), w, pair_s.at[p], pair_r.at[p], links.sibling)
        yield False
        links.remote(w, w, pair_s.at[p], pair_r.at[p], links.sibling).wait_recv()
        add_rows(w, 0, ((w, 0), (src, own_row)), part)
        base, bases, free = 0, [], 0
        for s in range(3):
            q = part // RING ** (s + 1)
            h = q // 2
            me = place[axes[s]]
            bases.append(base)
            here = base + me * q
            if s == 0 and ring_first:
                for d, sign in enumerate((1, -1)):
                    links.send(at(w, base + wrap(me + 2) * q + d * h, h), land.at[free + d * h : free + d * h + h, :],
                               *rs(s, d), links.along(axes[s], sign))
                yield False
                for d, sign in enumerate((1, -1)):
                    to = links.along(axes[s], sign)
                    row = base + wrap(me + sign) * q
                    half = land.at[free + d * h : free + d * h + h, :]
                    links.remote(half, half, *rs(s, d), to).wait_recv()
                    add_rows(w, row + d * h, ((w, row + d * h), (land, free + d * h)), h)
                    whole = land.at[free + (d + 1) * q : free + (d + 2) * q, :]
                    links.send(at(w, row, q), whole, *rs(s, 2 + d), to)
                yield False
                for d, sign in enumerate((1, -1)):
                    whole = land.at[free + (d + 1) * q : free + (d + 2) * q, :]
                    links.remote(whole, whole, *rs(s, 2 + d), links.along(axes[s], sign)).wait_recv()
                terms = ((w, here), (land, free + q), (land, free + 2 * q))
            else:
                for k in (2, 1, 3):
                    links.send(at(w, base + wrap(me + k) * q, q), land.at[free + (k - 1) * q : free + k * q, :],
                               *rs(s, k), links.along(axes[s], k))
                yield False
                for k in (1, 3, 2):
                    whole = land.at[free + (k - 1) * q : free + k * q, :]
                    links.remote(whole, whole, *rs(s, k), links.along(axes[s], k)).wait_recv()
                terms = ((w, here),) + tuple((land, free + i * q) for i in range(3))
            if s < 2:
                add_rows(w, here, terms, q)
            else:
                add_rows(last, 0, terms, q)
            base = here
            free += 3 * q
        keep_fin = pltpu.make_async_copy(last, result(base, q), fin_sem.at[p])
        keep_fin.start()
        for s in (2, 1, 0):
            q = part // RING ** (s + 1)
            h = q // 2
            me = place[axes[s]]
            block = result(bases[s] + me * q, q)
            if s == 0:
                links.send(block, block, back_s.at[p, 0], back_r.at[p, 0], links.sibling)
            if s == 0 and ring_first:
                for d, sign in enumerate((1, -1)):
                    links.send(block, block, *ag(s, d), links.along(axes[s], sign))
                yield False
                for d, sign in enumerate((1, -1)):
                    to = links.along(axes[s], sign)
                    row = bases[s] + wrap(me - sign) * q
                    block = result(row, q)
                    links.remote(block, block, *ag(s, d), to).wait_recv()
                    piece = result(row + d * h, h)
                    links.send(piece, piece, *ag(s, 2 + d), to)
                    links.send(block, block, back_s.at[p, 1 + d], back_r.at[p, 1 + d], links.sibling)
                yield False
                row = bases[s] + wrap(me + 2) * q
                for d, sign in enumerate((1, -1)):
                    piece = result(row + d * h, h)
                    links.remote(piece, piece, *ag(s, 2 + d), links.along(axes[s], sign)).wait_recv()
                block = result(row, q)
                links.send(block, block, back_s.at[p, 3], back_r.at[p, 3], links.sibling)
            else:
                for k in (2, 1, 3):
                    links.send(last if s == 2 else block, block, *ag(s, k), links.along(axes[s], k))
                yield False
                for i, k in enumerate((1, 3, 2)):
                    block = result(bases[s] + wrap(me - k) * q, q)
                    links.remote(block, block, *ag(s, k), links.along(axes[s], k)).wait_recv()
                    if s == 0:
                        links.send(block, block, back_s.at[p, 1 + i], back_r.at[p, 1 + i], links.sibling)
            if s == 2:
                keep_fin.wait()
        yield False
        for i, off in enumerate((0, -1, 1, 2)):
            piece = at(res, other_row + wrap(place[axes[0]] + off) * chunk, chunk)
            links.remote(piece, piece, back_s.at[p, i], back_r.at[p, i], links.sibling).wait_recv()
        yield True

    def alpha_job():
        links.send(ga, gr.at[3, 0], ga_s.at[3, 0], ga_r.at[3, 0], links.sibling)
        yield False
        links.remote(ga, gr.at[3, 0], ga_s.at[3, 0], ga_r.at[3, 0], links.sibling).wait_recv()
        gat[0] = ga[...] + gr[3, 0]
        for s in range(3):
            me = place[s]
            gr[s, me] = gat[s]
            for k in range(1, RING):
                links.send(gat.at[s], gr.at[s, me], ga_s.at[s, k], ga_r.at[s, k], links.along(s, k))
            yield False
            for k in range(1, RING):
                links.remote(gat.at[s], gr.at[s, wrap(me - k)], ga_s.at[s, k], ga_r.at[s, k],
                             links.along(s, k)).wait_recv()
            gat[s + 1] = (gr[s, 0] + gr[s, 1]) + (gr[s, 2] + gr[s, 3])
        fa_ref[...] = gat[3]
        yield True

    ends = []
    total = 0
    for r in range(REC):
        total = total + len_ref[0, r]
        ends.append(total * TILE)

    def rem_body(i, _):
        rows = pl.ds(pl.multiple_of(i * 32, 32), 32)
        p = lax.broadcasted_iota(jnp.int32, (32, 128), 0) + (i * 32 - LEAD + anchor)
        hi, lo = jnp.zeros_like(p), jnp.full_like(p, -1)
        start = 0
        for end in ends:
            inside = (p >= start) & (p < end)
            hi = jnp.where(inside, end - p, hi)
            lo = jnp.where(inside, p - start, lo)
            start = end
        rem[0, rows, :] = hi
        rem[1, rows, :] = lo
        return 0

    lax.fori_loop(0, rows_all // 32, rem_body, 0)

    for i in range(5):
        row = jnp.broadcast_to(al_ref[i : i + 1, :], (8, C))
        for h in range(2):
            kcol[0, i, h] = row[:, halves[h]] * (1.0 / 3.14159265358979)
            kcol[1, i, h] = 1.0 / row[:, halves[h]]
    acc[...] = jnp.zeros_like(acc)

    def four(x):
        return jnp.concatenate([x] * 4, axis=0)

    def activate(v, i, h):
        k0 = four(kcol[0, i, h])
        k1 = four(kcol[1, i, h])
        s2, sq = sine_parts(v * k0)
        q = sq * k1
        return v + q, s2, v * s2 - q

    class Totals:
        def __init__(self, i):
            self.i, self.sums = i, [None, None]

        def add(self, h, x):
            x = (x[0:8] + x[8:16]) + (x[16:24] + x[24:32])
            self.sums[h] = x if self.sums[h] is None else self.sums[h] + x

        def store(self):
            for h in range(2):
                if self.sums[h] is not None:
                    acc[self.i, h] += self.sums[h]

    def pieces(lo, hi):
        return [(slice(r, r + 32), r - lo, own0 <= r and r + 32 <= own1) for r in range(lo, hi, 32)]

    def row_loop(lo, hi, fn, group=4):
        cuts = sorted({lo, max(lo, own0), min(hi, own1), hi})
        for a, b in zip(cuts, cuts[1:]):
            own = a >= own0 and b <= own1
            many = group if ((b - a) // 32) % group == 0 else 1

            def step(i, _, own=own, a=a, many=many):
                for n in range(many):
                    fn(pl.ds(pl.multiple_of((i * many + n) * 32 + a, 16), 32), own)
                return 0

            lax.fori_loop(0, (b - a) // (32 * many), step, 0)

    def pipelined(span, blocks, product, use, mid=False):
        lo, hi = span
        count = (hi - lo) // 32
        starts = [lo + 32 * (count * n // blocks) for n in range(blocks + 1)]
        spans = list(zip(starts, starts[1:]))

        def make(n):
            a, b = spans[n]
            hbuf[n % 2, 0 : b - a, :] = product(slice(a, b))

        make(0)
        for n, (a, b) in enumerate(spans):
            if n + 1 < blocks:
                make(n + 1)
            use(pieces(a, b), hbuf.at[n % 2])
            if n == 1 and mid:
                tick()

    def forward_weights(unit):
        for k in range(TAPS):
            wt[k * C : (k + 1) * C, :] = wd_ref[unit, :, k * C : (k + 1) * C].T
        wpt[...] = wp_ref[unit].T

    def sig_body(j, _):
        src = pl.ds(pl.multiple_of(j * 512, 128), 512)
        u0[pl.ds(pl.multiple_of(j * 512 + own0, 16), 512), :] = sig_ref[:, src].T
        return 0

    lax.fori_loop(0, samples // 512, sig_body, 0)
    for o in range(2):
        gb[16 : 16 + rows_j, o * C : (o + 1) * C] = og_ref[o * C : (o + 1) * C, :].T

    links.met()
    halo = []
    for i, (ref, count, first, last) in enumerate(((u0, 80, own0, own1), (gb, 16, 16, 16 + rows_j))):
        for side, (step, src, dst) in enumerate(((-1, first, last), (1, last - count, first - count))):
            n = 2 * i + side
            halo.append(links.remote(ref.at[src : src + count, :], ref.at[dst : dst + count, :],
                                     halo_s.at[n], halo_r.at[n], links.in_time(step)))
    for copy in halo:
        copy.start()
    for h in range(2):
        af[h][...] = jnp.zeros_like(af[h])
        df[h][...] = jnp.zeros_like(df[h])
    forward_weights(0)
    for copy in halo:
        copy.wait()

    def keep(i, rows, h, s2, t):
        slope[i, rows, halves[h]] = (1.0 + s2).astype(BF16)
        sa[i, rows, halves[h]] = t.astype(BF16)

    def first(rows, own):
        alive = rem[0, rows, :] > 0
        for h in range(2):
            v = jnp.where(alive, u0[rows, halves[h]].astype(F32), 0.0)
            u0[rows, halves[h]] = v.astype(BF16)
            a, s2, t = activate(v, 0, h)
            af[h][rows, :] = a
            a0[rows, halves[h]] = a.astype(BF16)
            keep(0, rows, h, s2, t)

    row_loop(own0 - 64 - 32, own1 + 64 + 32, first)

    def shift_pass(unit, span):
        d = DILATIONS[unit]
        lo, hi = span

        def step(i, _):
            start = i * 32 + lo
            rows = pl.ds(pl.multiple_of(start, 16), 32)
            after, before = rem[0, rows, :], rem[1, rows, :]
            for k in range(TAPS):
                by = (k - TAPS // 2) * d
                for h in range(2):
                    x = af[h][pl.ds(start + by, 32), :]
                    if by > 0:
                        x = jnp.where(after > by, x, 0.0)
                    elif by < 0:
                        x = jnp.where(before >= -by, x, 0.0)
                    cols[rows, k * C + h * 128 : k * C + h * 128 + 128] = x.astype(BF16)
            return 0

        lax.fori_loop(0, (hi - lo) // 32, step, 0)

    def forward(unit):
        b_ref, u_ref = b_of[unit], u_of[unit]
        hi, ui = 2 * unit + 1, 2 * unit + 2
        def hidden(parts, buf):
            for r, o, own in parts:
                for h in range(2):
                    a, s2, t = activate(buf[o : o + 32, halves[h]], hi, h)
                    b_ref[r, halves[h]] = a.astype(BF16)
                    keep(hi, r, h, s2, t)

        pipelined(wide, 4, lambda rows: dot(cols[rows, :], wt[...]), hidden)

        def outer(parts, buf):
            for r, o, own in parts:
                for h in range(2):
                    u = (u_ref[r, halves[h]].astype(F32) + buf[o : o + 32, halves[h]]).astype(BF16)
                    if unit == 0:
                        u1[r, halves[h]] = u
                    a, s2, t = activate(u.astype(F32), ui, h)
                    af[h][r, :] = a
                    keep(ui, r, h, s2, t)

        pipelined(wide, 4, lambda rows: dot(b_ref[rows, :], wpt[...]), outer)

    shift_pass(0, wide)
    forward(0)
    forward_weights(1)
    shift_pass(1, wide)
    forward(1)

    at_j = pl.ds(own0, rows_j, stride=STRIDE)
    after, before = rem[0, at_j, :], rem[1, at_j, :]
    for k in range(2 * STRIDE):
        by = k - STRIDE // 2
        for h in range(2):
            z = af[h][pl.ds(own0 + by, rows_j, stride=STRIDE), :]
            if by < 0:
                z = jnp.where(before >= -by, z, 0.0)
            elif by >= STRIDE:
                z = jnp.where(after > by, z, 0.0)
            zcols[k, :, halves[h]] = z.astype(BF16)

    gtf[8 : 8 + rows_j + 32, :] = gb[...].astype(F32)
    at_m = pl.ds(wide[0], all_j, stride=STRIDE)
    after, before = rem[0, at_m, :], rem[1, at_m, :]
    for o in range(4):
        lanes = slice(o * 128, o * 128 + 128)
        gt[0, :, lanes] = jnp.where(after > 0, gtf[16 : 16 + all_j, lanes], 0.0).astype(BF16)
        gt[1, :, lanes] = jnp.where(before > 0, gtf[15 : 15 + all_j, lanes], 0.0).astype(BF16)
        gt[2, :, lanes] = jnp.where(after > STRIDE, gtf[17 : 17 + all_j, lanes], 0.0).astype(BF16)

    load.wait()

    own = og_ref[...]

    def down_body(k, _):
        d = dot(own, zcols[k]).astype(BF16)
        for h in range(2):
            gdn[pl.ds(pl.multiple_of((2 * k + h) * 2 * C, 16), 2 * C), :] = d[:, halves[h]]
        return 0

    lax.fori_loop(0, 2 * STRIDE, down_body, 0)
    for p in range(4):
        jobs.append(job(p))
    tick()

    for o in range(2):
        rows = slice(o * C, (o + 1) * C)
        total = dot_nt(wdn_ref[0, rows, :], zcols[0])
        for k in range(1, 2 * STRIDE):
            total = total + dot_nt(wdn_ref[k, rows, :], zcols[k])
        out_ref[rows, :] = total.astype(BF16)
    tick()

    for p in range(STRIDE):
        if p < STRIDE // 2:
            d = dot(gt[1], wdn_ref[p + 12])
        else:
            d = dot(gt[2], wdn_ref[p - 4])
        d = d + dot(gt[0], wdn_ref[p + 4])
        for h in range(2):
            df[h][pl.ds(wide[0] + p, all_j, stride=STRIDE), :] = d[:, halves[h]]
    tick()

    sums = Totals(4)
    for r, _, own_piece in pieces(*wide):
        for h in range(2):
            dz = df[h][r, :]
            grad[r, halves[h]] = (dz * slope[4, r, halves[h]].astype(F32)).astype(BF16)
            if own_piece:
                sums.add(h, dz * sa[4, r, halves[h]].astype(F32))
    sums.store()

    def transposed(j, _):
        lanes = pl.ds(pl.multiple_of(j * 512, 128), 512)
        tr[:, lanes] = grad[pl.ds(pl.multiple_of(j * 512 + own0, 16), 512), :].T
        return 0

    def transposed_e(j, _):
        lanes = pl.ds(pl.multiple_of(j * 512, 128), 512)
        rows = pl.ds(pl.multiple_of(j * 512 + own0, 16), 512)
        for h in range(2):
            tr[halves[h], lanes] = af[h][rows, :].astype(BF16).T
        return 0

    def put_gw(unit, k, x):
        for h in range(2):
            first = ((unit * (TAPS + 1) + k) * 2 + h) * C
            gw[first : first + C, :] = x[:, halves[h]].astype(BF16)

    def backward(unit):
        b_ref = b_of[unit]
        hi, ui = 2 * unit + 1, 2 * unit
        span = (near, wide)[unit]
        lax.fori_loop(0, samples // 512, transposed, 0)
        put_gw(unit, TAPS, dot(tr[...], b_ref[own0:own1, :]))
        if unit == 1:
            tick()
        if unit == 0:

            def again(rows, own):
                for h in range(2):
                    af[h][rows, :] = a0[rows, halves[h]].astype(F32)

            row_loop(*near, again)
            shift_pass(0, own_rows)
            tick()

        def hidden(parts, buf):
            sums = Totals(hi)
            for r, o, own in parts:
                for h in range(2):
                    c = buf[o : o + 32, halves[h]]
                    af[h][r, :] = c * slope[hi, r, halves[h]].astype(F32)
                    if own:
                        sums.add(h, c * sa[hi, r, halves[h]].astype(F32))
            sums.store()

        pipelined(span, 4, lambda rows: dot(grad[rows, :], wp_ref[unit]), hidden)
        tick()
        lax.fori_loop(0, samples // 512, transposed_e, 0)

        for k in range(TAPS):
            put_gw(unit, k, dot(tr[...], cols[own0:own1, k * C : (k + 1) * C]))
        jobs.append(job(4 + 2 * unit))
        jobs.append(job(5 + 2 * unit))
        tick()

        span = (own_rows, near)[unit]
        for k in range(TAPS):
            wt[k * C : (k + 1) * C, :] = wd_ref[unit, :, (TAPS - 1 - k) * C : (TAPS - k) * C]
        shift_pass(unit, span)

        def inner(parts, buf):
            sums = Totals(ui)
            for r, o, own in parts:
                for h in range(2):
                    f = buf[o : o + 32, halves[h]]
                    g = grad[r, halves[h]].astype(F32) + f * slope[ui, r, halves[h]].astype(F32)
                    if unit == 0:
                        g = jnp.where(rem[0, r, :] > 0, g, 0.0)
                    grad[r, halves[h]] = g.astype(BF16)
                    if own:
                        sums.add(h, f * sa[ui, r, halves[h]].astype(F32))
            sums.store()

        pipelined(span, 4, lambda rows: dot(cols[rows, :], wt[...]), inner, mid=True)
        tick()

    backward(1)
    backward(0)

    ga[...] = jnp.zeros_like(ga)
    for i in range(5):
        for h in range(2):
            ga[i : i + 1, halves[h]] = jnp.sum(acc[i, h] * kcol[1, i, h], axis=0, keepdims=True)
    jobs.append(alpha_job())
    tick()

    def sg_body(j, _):
        lanes = pl.ds(pl.multiple_of(j * 512, 128), 512)
        sg_ref[:, lanes] = grad[pl.ds(pl.multiple_of(j * 512 + own0, 16), 512), :].T
        return 0

    lax.fori_loop(0, samples // 512, sg_body, 0)
    while jobs:
        tick()
    links.drain()


def block_and_sums(lengths, sig, og, conv_dilated, conv_point, conv_down, snake_alpha):
    samples = sig.shape[1]
    rows = samples + 2 * LEAD
    rows_j = samples // STRIDE
    vmem = pl.BlockSpec(memory_space=pltpu.VMEM)
    anywhere = pl.BlockSpec(memory_space=pl.ANY)
    dma = pltpu.SemaphoreType.DMA
    n_jobs = len(ORDERS)

    def landing(count):
        return sum(3 * (count // RING ** (s + 1)) for s in range(3))

    outs = (
        jax.ShapeDtypeStruct((2 * C, rows_j), BF16),
        jax.ShapeDtypeStruct((C, samples), BF16),
        jax.ShapeDtypeStruct((8 * JOB_ROWS[0], 128), BF16),
        jax.ShapeDtypeStruct((8 * JOB_ROWS[4], 128), BF16),
        jax.ShapeDtypeStruct((8, C), F32),
    )
    scratch = [
        pltpu.VMEM((rows, TAPS * C), BF16),
        pltpu.VMEM((rows, 128), F32),
        pltpu.VMEM((rows, 128), F32),
        pltpu.VMEM((rows, 128), F32),
        pltpu.VMEM((rows, 128), F32),
        pltpu.VMEM((rows, C), BF16),
        pltpu.VMEM((rows, C), BF16),
        pltpu.VMEM((rows, C), BF16),
        pltpu.VMEM((rows, C), BF16),
        pltpu.VMEM((rows, C), BF16),
        pltpu.VMEM((rows, C), BF16),
        pltpu.VMEM((5, rows, C), BF16),
        pltpu.VMEM((5, rows, C), BF16),
        pltpu.VMEM((C, samples), BF16),
        pltpu.VMEM((2 * STRIDE, rows_j, C), BF16),
        pltpu.VMEM((rows_j + 32, 2 * C), BF16),
        pltpu.VMEM((rows_j + 48, 2 * C), F32),
        pltpu.VMEM((3, rows_j + 16, 2 * C), BF16),
        pltpu.VMEM((TAPS * C, C), BF16),
        pltpu.VMEM((C, C), BF16),
        pltpu.VMEM((2, rows, 128), jnp.int32),
        pltpu.VMEM((2, 5, 2, 8, 128), F32),
        pltpu.VMEM((5, 2, 8, 128), F32),
        pltpu.VMEM((2, 544, C), F32),
        pltpu.VMEM(conv_down.shape, BF16),
        pltpu.VMEM((8 * JOB_ROWS[0], 128), BF16),
        pltpu.VMEM((8 * JOB_ROWS[4], 128), BF16),
        pltpu.VMEM((8, C), F32),
        pltpu.VMEM((4, JOB_ROWS[0], 128), BF16),
        pltpu.VMEM((4, JOB_ROWS[4], 128), BF16),
        pltpu.VMEM((4, landing(JOB_ROWS[0]), 128), BF16),
        pltpu.VMEM((4, landing(JOB_ROWS[4]), 128), BF16),
        pltpu.VMEM((n_jobs, JOB_ROWS[0] // RING**3, 128), BF16),
        pltpu.VMEM((4, RING, 8, C), F32),
        pltpu.VMEM((4, 8, C), F32),
        dma, dma((4,)), dma((4,)), dma((n_jobs,)), dma((n_jobs,)),
        dma((12 * n_jobs,)), dma((12 * n_jobs,)), dma((12 * n_jobs,)), dma((12 * n_jobs,)),
        dma((n_jobs,)), dma((n_jobs, 4)), dma((n_jobs, 4)), dma((4, RING)), dma((4, RING)),
    ]
    return pl.pallas_call(
        functools.partial(block_kernel, samples),
        out_shape=outs,
        in_specs=[pl.BlockSpec(memory_space=pltpu.SMEM)] + [vmem] * 4 + [anywhere, vmem],
        out_specs=(vmem, vmem, anywhere, anywhere, vmem),
        scratch_shapes=scratch,
        compiler_params=pltpu.CompilerParams(
            collective_id=1, has_side_effects=True, vmem_limit_bytes=63 * 1024 * 1024
        ),
        name="encoder_block",
    )(lengths, sig, og, conv_dilated, conv_point, conv_down, snake_alpha)


def widen_kernel(dn_ref, w_ref, out_in, sg_in, ga_in, gdn_ref, gd_ref, gp_ref, out_ref, sg_ref, ga_ref,
                 dn, w, wide_dn, wide_w, in_sem, out_sem, pass_sem):
    passing = [pltpu.make_async_copy(a, b, pass_sem.at[i])
               for i, (a, b) in enumerate(((out_in, out_ref), (sg_in, sg_ref), (ga_in, ga_ref)))]
    steps = 2 * STRIDE
    ins = []
    for i in range(steps):
        d, g = slice(i * 4 * C, (i + 1) * 4 * C), slice(i * 2 * C, (i + 1) * 2 * C)
        ins.append((pltpu.make_async_copy(dn_ref.at[d, :], dn.at[d, :], in_sem.at[0, i]),
                    pltpu.make_async_copy(w_ref.at[g, :], w.at[g, :], in_sem.at[1, i])))
        for copy in ins[-1]:
            copy.start()
    for copy in passing:
        copy.start()
    outs = []
    for i in range(steps):
        unit, k = divmod(i, TAPS + 1)
        for copy in ins[i]:
            copy.wait()
        for h in range(2):
            lanes = slice(h * 128, h * 128 + 128)
            wide_dn[i, :, lanes] = dn[(2 * i + h) * 2 * C : (2 * i + h + 1) * 2 * C, :].astype(F32)
            wide_w[i, :, lanes] = w[(2 * i + h) * C : (2 * i + h + 1) * C, :].astype(F32)
        to = gd_ref.at[unit, :, k * C : (k + 1) * C] if k < TAPS else gp_ref.at[unit]
        outs += [pltpu.make_async_copy(wide_dn.at[i], gdn_ref.at[i], out_sem.at[0, i]),
                 pltpu.make_async_copy(wide_w.at[i], to, out_sem.at[1, i])]
        outs[-2].start()
        outs[-1].start()
    for copy in outs + passing:
        copy.wait()


def widen(fdn, fw, out, sg, ga):
    steps = 2 * STRIDE
    anywhere = pl.BlockSpec(memory_space=pl.ANY)
    dma = pltpu.SemaphoreType.DMA
    return pl.pallas_call(
        widen_kernel,
        out_shape=(
            jax.ShapeDtypeStruct((steps, 2 * C, C), F32),
            jax.ShapeDtypeStruct((2, C, TAPS * C), F32),
            jax.ShapeDtypeStruct((2, C, C), F32),
            jax.ShapeDtypeStruct(out.shape, out.dtype),
            jax.ShapeDtypeStruct(sg.shape, sg.dtype),
            jax.ShapeDtypeStruct(ga.shape, ga.dtype),
        ),
        in_specs=[anywhere] * 5,
        out_specs=(anywhere,) * 6,
        scratch_shapes=[
            pltpu.VMEM(fdn.shape, BF16),
            pltpu.VMEM(fw.shape, BF16),
            pltpu.VMEM((steps, 2 * C, C), F32),
            pltpu.VMEM((steps, C, C), F32),
            dma((2, steps)), dma((2, steps)), dma((3,)),
        ],
        compiler_params=pltpu.CompilerParams(vmem_limit_bytes=63 * 1024 * 1024),
        name="widen",
    )(fdn, fw, out, sg, ga)


def body(signal, lengths, conv_dilated, conv_point, conv_down, snake_alpha, out_grad):
    out, sg, fdn, fw, ga = block_and_sums(
        lengths, signal[0], out_grad[0], conv_dilated, conv_point, conv_down, snake_alpha
    )
    gdn, gd, gp, out, sg, ga = widen(fdn, fw, out, sg, ga)
    return (out[None], sg[None], gd, gp, gdn, ga[:5])


def solution(mesh):
    placed = (P("dp", None, "tm"), P("dp", None), P(), P(), P(), P(), P("dp", None, "tm"))
    return jax.shard_map(
        body,
        mesh=mesh,
        in_specs=placed,
        out_specs=(P("dp", None, "tm"), P("dp", None, "tm"), P(), P(), P(), P()),
        check_vma=False,
    )
```

profile of v0, /device:TPU:1, one launch (start us, length us, event | category | flops | bytes accessed | tf_op | source)
XLA Modules:
  0.0 163.3 jit_solution(5395946668775615529)
XLA Ops:
  0.6 120.8 %encoder_block.1 = (bf16[512,256]{1,0:T(8,128)(2,1)}, bf16[256,2048]{1,0:T(8,128)(2,1)}, bf16[16384,128]{1,0:T(8,128)(2,1)}, bf16[8192,128]{1,0:T(8,128)(2,1)}, f32[8,256]{1,0:T(8,128)}) custom-call(s32[1,5]{1,0:T(1,128)} %len_ref.1, bf16[256,2048]{1,0:T(8,128)(2,1)} %bitcast.5, bf16[512,256]{1,0:T(8,128)(2,1)} %bitcast.6, bf16[2,256,1792]{2,1,0:T(8,128)(2,1)} %wd_ref.1, ...), custom_call_target="tpu_custom_call" | custom-call | tf_op jit(solution)/shard_map/encoder_block/pallas_call | solution.py:683
  121.5 41.7 %widen.1 = (f32[16,512,256]{2,1,0:T(8,128)}, f32[2,256,1792]{2,1,0:T(8,128)}, f32[2,256,256]{2,1,0:T(8,128)}, bf16[512,256]{1,0:T(8,128)(2,1)}, bf16[256,2048]{1,0:T(8,128)(2,1)}, /*index=5*/f32[8,256]{1,0:T(8,128)}) custom-call(bf16[16384,128]{1,0:T(8,128)(2,1)} %get-tuple-element.17.dn_ref, bf16[8192,128]{1,0:T(8,128)(2,1)} %get-tuple-element.18.w_ref, ...), custom_call_target="tpu_custom_call" | custom-call | tf_op jit(solution)/shard_map/widen/pallas_call | solution.py:732
where the time goes:
time: 163 us
  Pallas kernels  163 us (100%)
    pallas_call x1, Pallas kernels, block_and_sums(): pl.pallas_call(functools.partial(block_kernel, samples), out_shape=outs,...  121 us
    pallas_call x1, Pallas kernels, widen(): pl.pallas_call(widen_kernel, out_shape=(jax.ShapeDtypeStruct((steps, 2 *...  41.7 us

commit v1 on v0

--- a/solution.py
+++ b/solution.py
@@ -45,8 +45,10 @@
 
 RING = 4
 MESH = pl.DeviceIdType.MESH
-ORDERS = ((0, 1, 2), (1, 2, 0), (2, 0, 1), (0, 2, 1), (1, 2, 0), (2, 0, 1), (1, 2, 0), (2, 0, 1))
-JOB_ROWS = (2048,) * 4 + (1024,) * 4
+ORDERS = ((0, 1, 2), (1, 2, 0), (2, 0, 1), (1, 2, 0), (2, 0, 1), (0, 1, 2), (2, 1, 0))
+N_DOWN = 3
+UNIT_OF = (0, 0, 1, 1)
+JOB_ROWS = (3072, 3072, 2048) + (1024,) * 4
 
 
 class Links:
@@ -99,13 +101,17 @@
                  out_ref, sg_ref, fdn_ref, fw_ref, fa_ref,
                  cols, af0, af1, df0, df1, u0, u1, a0, b0, b1, grad, slope, sa, tr, zcols,
                  gb, gtf, gt, wt, wpt, rem, kcol, acc, hbuf, wdn_ref, gdn, gw, ga,
-                 pr_dn, pr_w, land_dn, land_w, fin, gr, gat,
+                 pr, lands, fin, gr, gat,
                  load_sem, halo_s, halo_r, pair_s, pair_r, rs_s, rs_r, ag_s, ag_r, fin_sem, back_s, back_r, ga_s, ga_r):
     load = pltpu.make_async_copy(wdn_hbm, wdn_ref, load_sem)
     load.start()
     links = Links()
     links.greet()
     jobs = []
+
+    def start(job):
+        next(job)
+        jobs.append(job)
 
     def tick():
         for job in list(jobs):
@@ -128,10 +134,12 @@
     place = links.place
 
     def job_rows(p, hf):
-        if p < 4:
-            return gdn, fdn_ref, hf * 4 * JOB_ROWS[0] + p * JOB_ROWS[0]
-        unit, sub = (p - 4) // 2, (p - 4) % 2
-        return gw, fw_ref, (unit * 4 + hf * 2 + sub) * JOB_ROWS[4]
+        if p < N_DOWN:
+            return gdn, fdn_ref, hf * sum(JOB_ROWS[:N_DOWN]) + sum(JOB_ROWS[:p])
+        unit = UNIT_OF[p - N_DOWN]
+        before = sum(JOB_ROWS[q] for q in range(N_DOWN, p) if UNIT_OF[q - N_DOWN] == unit)
+        half = sum(JOB_ROWS[q] for q in range(N_DOWN, len(ORDERS)) if UNIT_OF[q - N_DOWN] == unit)
+        return gw, fw_ref, unit * 2 * half + hf * half + before
 
     def at(ref, start, count):
         return ref.at[pl.ds(pl.multiple_of(start, 16), count), :]
@@ -140,7 +148,7 @@
         return lax.rem(c + RING, RING)
 
     def add_rows(dst, d0, terms, count):
-        step_rows = min(count, 128)
+        step_rows = next(n for n in (256, 128, 96, 64, 48, 32, 16) if count % n == 0)
 
         def one(i, _):
             v = None
@@ -158,9 +166,10 @@
         chunk = part // RING
         src, res, other_row = job_rows(p, 1 - core)
         own_row = job_rows(p, core)[2]
-        w, land = (pr_dn.at[p], land_dn.at[p]) if p < 4 else (pr_w.at[p - 4], land_w.at[p - 4])
+        offset = sum(JOB_ROWS[:p])
+        w, land = pr.at[offset : offset + part, :], lands.at[offset : offset + part, :]
         last = fin.at[p, 0 : part // RING**3, :]
-        ring_first = p < 4
+        ring_first = p < N_DOWN
 
         def result(row, count):
             return at(res, own_row + row, count)
@@ -222,7 +231,7 @@
             h = q // 2
             me = place[axes[s]]
             block = result(bases[s] + me * q, q)
-            if s == 0:
+            if s == 0 and not ring_first:
                 links.send(block, block, back_s.at[p, 0], back_r.at[p, 0], links.sibling)
             if s == 0 and ring_first:
                 for d, sign in enumerate((1, -1)):
@@ -235,14 +244,13 @@
                     links.remote(block, block, *ag(s, d), to).wait_recv()
                     piece = result(row + d * h, h)
                     links.send(piece, piece, *ag(s, 2 + d), to)
-                    links.send(block, block, back_s.at[p, 1 + d], back_r.at[p, 1 + d], links.sibling)
                 yield False
                 row = bases[s] + wrap(me + 2) * q
                 for d, sign in enumerate((1, -1)):
                     piece = result(row + d * h, h)
                     links.remote(piece, piece, *ag(s, 2 + d), links.along(axes[s], sign)).wait_recv()
-                block = result(row, q)
-                links.send(block, block, back_s.at[p, 3], back_r.at[p, 3], links.sibling)
+                block = result(0, part)
+                links.send(block, block, back_s.at[p, 0], back_r.at[p, 0], links.sibling)
             else:
                 for k in (2, 1, 3):
                     links.send(last if s == 2 else block, block, *ag(s, k), links.along(axes[s], k))
@@ -255,9 +263,13 @@
             if s == 2:
                 keep_fin.wait()
         yield False
-        for i, off in enumerate((0, -1, 1, 2)):
-            piece = at(res, other_row + wrap(place[axes[0]] + off) * chunk, chunk)
-            links.remote(piece, piece, back_s.at[p, i], back_r.at[p, i], links.sibling).wait_recv()
+        if ring_first:
+            block = at(res, other_row, part)
+            links.remote(block, block, back_s.at[p, 0], back_r.at[p, 0], links.sibling).wait_recv()
+        else:
+            for i, off in enumerate((0, -1, 1, 2)):
+                block = at(res, other_row + wrap(place[axes[0]] + off) * chunk, chunk)
+                links.remote(block, block, back_s.at[p, i], back_r.at[p, i], links.sibling).wait_recv()
         yield True
 
     def alpha_job():
@@ -346,7 +358,7 @@
 
             lax.fori_loop(0, (b - a) // (32 * many), step, 0)
 
-    def pipelined(span, blocks, product, use, mid=False):
+    def pipelined(span, blocks, product, use):
         lo, hi = span
         count = (hi - lo) // 32
         starts = [lo + 32 * (count * n // blocks) for n in range(blocks + 1)]
@@ -361,8 +373,6 @@
             if n + 1 < blocks:
                 make(n + 1)
             use(pieces(a, b), hbuf.at[n % 2])
-            if n == 1 and mid:
-                tick()
 
     def forward_weights(unit):
         for k in range(TAPS):
@@ -378,21 +388,10 @@
     for o in range(2):
         gb[16 : 16 + rows_j, o * C : (o + 1) * C] = og_ref[o * C : (o + 1) * C, :].T
 
-    links.met()
-    halo = []
-    for i, (ref, count, first, last) in enumerate(((u0, 80, own0, own1), (gb, 16, 16, 16 + rows_j))):
-        for side, (step, src, dst) in enumerate(((-1, first, last), (1, last - count, first - count))):
-            n = 2 * i + side
-            halo.append(links.remote(ref.at[src : src + count, :], ref.at[dst : dst + count, :],
-                                     halo_s.at[n], halo_r.at[n], links.in_time(step)))
-    for copy in halo:
-        copy.start()
     for h in range(2):
         af[h][...] = jnp.zeros_like(af[h])
         df[h][...] = jnp.zeros_like(df[h])
     forward_weights(0)
-    for copy in halo:
-        copy.wait()
 
     def keep(i, rows, h, s2, t):
         slope[i, rows, halves[h]] = (1.0 + s2).astype(BF16)
@@ -408,9 +407,9 @@
             a0[rows, halves[h]] = a.astype(BF16)
             keep(0, rows, h, s2, t)
 
-    row_loop(own0 - 64 - 32, own1 + 64 + 32, first)
-
-    def shift_pass(unit, span):
+    row_loop(*own_rows, first)
+
+    def shift_pass(unit, span, src=af):
         d = DILATIONS[unit]
         lo, hi = span
 
@@ -421,7 +420,7 @@
             for k in range(TAPS):
                 by = (k - TAPS // 2) * d
                 for h in range(2):
-                    x = af[h][pl.ds(start + by, 32), :]
+                    x = src[h][pl.ds(start + by, 32), :]
                     if by > 0:
                         x = jnp.where(after > by, x, 0.0)
                     elif by < 0:
@@ -431,7 +430,7 @@
 
         lax.fori_loop(0, (hi - lo) // 32, step, 0)
 
-    def forward(unit):
+    def forward(unit, span, blocks, dst):
         b_ref, u_ref = b_of[unit], u_of[unit]
         hi, ui = 2 * unit + 1, 2 * unit + 2
         def hidden(parts, buf):
@@ -441,7 +440,7 @@
                     b_ref[r, halves[h]] = a.astype(BF16)
                     keep(hi, r, h, s2, t)
 
-        pipelined(wide, 4, lambda rows: dot(cols[rows, :], wt[...]), hidden)
+        pipelined(span, blocks, lambda rows: dot(cols[rows, :], wt[...]), hidden)
 
         def outer(parts, buf):
             for r, o, own in parts:
@@ -450,16 +449,34 @@
                     if unit == 0:
                         u1[r, halves[h]] = u
                     a, s2, t = activate(u.astype(F32), ui, h)
-                    af[h][r, :] = a
+                    dst[h][r, :] = a
                     keep(ui, r, h, s2, t)
 
-        pipelined(wide, 4, lambda rows: dot(b_ref[rows, :], wpt[...]), outer)
-
-    shift_pass(0, wide)
-    forward(0)
+        pipelined(span, blocks, lambda rows: dot(b_ref[rows, :], wpt[...]), outer)
+
+    inner_rows = (own0 + 64, own1 - 64)
+    shift_pass(0, inner_rows)
+    forward(0, inner_rows, 4, df)
+
+    links.met()
+    halo = []
+    for i, (ref, count, lo, hi) in enumerate(((u0, 80, own0, own1), (gb, 16, 16, 16 + rows_j))):
+        for side, (step, src, dst) in enumerate(((-1, lo, hi), (1, hi - count, lo - count))):
+            n = 2 * i + side
+            halo.append(links.remote(ref.at[src : src + count, :], ref.at[dst : dst + count, :],
+                                     halo_s.at[n], halo_r.at[n], links.in_time(step)))
+    for copy in halo:
+        copy.start()
+    for copy in halo:
+        copy.wait()
+    for lo, hi in ((own0 - 96, own0), (own1, own1 + 96)):
+        row_loop(lo, hi, first)
+    for span in ((wide[0], inner_rows[0]), (inner_rows[1], wide[1])):
+        shift_pass(0, span)
+        forward(0, span, 1, df)
     forward_weights(1)
-    shift_pass(1, wide)
-    forward(1)
+    shift_pass(1, wide, df)
+    forward(1, wide, 4, af)
 
     at_j = pl.ds(own0, rows_j, stride=STRIDE)
     after, before = rem[0, at_j, :], rem[1, at_j, :]
@@ -493,9 +510,8 @@
         return 0
 
     lax.fori_loop(0, 2 * STRIDE, down_body, 0)
-    for p in range(4):
-        jobs.append(job(p))
-    tick()
+    for p in range(N_DOWN):
+        start(job(p))
 
     for o in range(2):
         rows = slice(o * C, (o + 1) * C)
@@ -503,7 +519,6 @@
         for k in range(1, 2 * STRIDE):
             total = total + dot_nt(wdn_ref[k, rows, :], zcols[k])
         out_ref[rows, :] = total.astype(BF16)
-    tick()
 
     for p in range(STRIDE):
         if p < STRIDE // 2:
@@ -513,7 +528,6 @@
         d = d + dot(gt[0], wdn_ref[p + 4])
         for h in range(2):
             df[h][pl.ds(wide[0] + p, all_j, stride=STRIDE), :] = d[:, halves[h]]
-    tick()
 
     sums = Totals(4)
     for r, _, own_piece in pieces(*wide):
@@ -523,6 +537,7 @@
             if own_piece:
                 sums.add(h, dz * sa[4, r, halves[h]].astype(F32))
     sums.store()
+    tick()
 
     def transposed(j, _):
         lanes = pl.ds(pl.multiple_of(j * 512, 128), 512)
@@ -547,8 +562,6 @@
         span = (near, wide)[unit]
         lax.fori_loop(0, samples // 512, transposed, 0)
         put_gw(unit, TAPS, dot(tr[...], b_ref[own0:own1, :]))
-        if unit == 1:
-            tick()
         if unit == 0:
 
             def again(rows, own):
@@ -557,7 +570,6 @@
 
             row_loop(*near, again)
             shift_pass(0, own_rows)
-            tick()
 
         def hidden(parts, buf):
             sums = Totals(hi)
@@ -575,9 +587,11 @@
 
         for k in range(TAPS):
             put_gw(unit, k, dot(tr[...], cols[own0:own1, k * C : (k + 1) * C]))
-        jobs.append(job(4 + 2 * unit))
-        jobs.append(job(5 + 2 * unit))
-        tick()
+        for p, of in enumerate(UNIT_OF):
+            if of == unit:
+                start(job(N_DOWN + p))
+        if unit == 0:
+            tick()
 
         span = (own_rows, near)[unit]
         for k in range(TAPS):
@@ -597,7 +611,7 @@
                         sums.add(h, f * sa[ui, r, halves[h]].astype(F32))
             sums.store()
 
-        pipelined(span, 4, lambda rows: dot(cols[rows, :], wt[...]), inner, mid=True)
+        pipelined(span, 4, lambda rows: dot(cols[rows, :], wt[...]), inner)
         tick()
 
     backward(1)
@@ -607,8 +621,7 @@
     for i in range(5):
         for h in range(2):
             ga[i : i + 1, halves[h]] = jnp.sum(acc[i, h] * kcol[1, i, h], axis=0, keepdims=True)
-    jobs.append(alpha_job())
-    tick()
+    start(alpha_job())
 
     def sg_body(j, _):
         lanes = pl.ds(pl.multiple_of(j * 512, 128), 512)
@@ -629,15 +642,11 @@
     anywhere = pl.BlockSpec(memory_space=pl.ANY)
     dma = pltpu.SemaphoreType.DMA
     n_jobs = len(ORDERS)
-
-    def landing(count):
-        return sum(3 * (count // RING ** (s + 1)) for s in range(3))
-
     outs = (
         jax.ShapeDtypeStruct((2 * C, rows_j), BF16),
         jax.ShapeDtypeStruct((C, samples), BF16),
-        jax.ShapeDtypeStruct((8 * JOB_ROWS[0], 128), BF16),
-        jax.ShapeDtypeStruct((8 * JOB_ROWS[4], 128), BF16),
+        jax.ShapeDtypeStruct((2 * sum(JOB_ROWS[:N_DOWN]), 128), BF16),
+        jax.ShapeDtypeStruct((2 * sum(JOB_ROWS[N_DOWN:]), 128), BF16),
         jax.ShapeDtypeStruct((8, C), F32),
     )
     scratch = [
@@ -666,13 +675,11 @@
         pltpu.VMEM((5, 2, 8, 128), F32),
         pltpu.VMEM((2, 544, C), F32),
         pltpu.VMEM(conv_down.shape, BF16),
-        pltpu.VMEM((8 * JOB_ROWS[0], 128), BF16),
-        pltpu.VMEM((8 * JOB_ROWS[4], 128), BF16),
+        pltpu.VMEM((2 * sum(JOB_ROWS[:N_DOWN]), 128), BF16),
+        pltpu.VMEM((2 * sum(JOB_ROWS[N_DOWN:]), 128), BF16),
         pltpu.VMEM((8, C), F32),
-        pltpu.VMEM((4, JOB_ROWS[0], 128), BF16),
-        pltpu.VMEM((4, JOB_ROWS[4], 128), BF16),
-        pltpu.VMEM((4, landing(JOB_ROWS[0]), 128), BF16),
-        pltpu.VMEM((4, landing(JOB_ROWS[4]), 128), BF16),
+        pltpu.VMEM((sum(JOB_ROWS), 128), BF16),
+        pltpu.VMEM((sum(JOB_ROWS), 128), BF16),
         pltpu.VMEM((n_jobs, JOB_ROWS[0] // RING**3, 128), BF16),
         pltpu.VMEM((4, RING, 8, C), F32),
         pltpu.VMEM((4, 8, C), F32),
@@ -694,9 +701,9 @@
 
 
 def widen_kernel(dn_ref, w_ref, out_in, sg_in, ga_in, gdn_ref, gd_ref, gp_ref, out_ref, sg_ref, ga_ref,
-                 dn, w, wide_dn, wide_w, in_sem, out_sem, pass_sem):
-    passing = [pltpu.make_async_copy(a, b, pass_sem.at[i])
-               for i, (a, b) in enumerate(((out_in, out_ref), (sg_in, sg_ref), (ga_in, ga_ref)))]
+                 dn, w, wide_dn, wide_w, out_v, sg_v, ga_v, in_sem, out_sem, pass_sem):
+    through = ((out_in, out_v, out_ref), (sg_in, sg_v, sg_ref), (ga_in, ga_v, ga_ref))
+    passing = [pltpu.make_async_copy(a, v, pass_sem.at[0, i]) for i, (a, v, _) in enumerate(through)]
     steps = 2 * STRIDE
     ins = []
     for i in range(steps):
@@ -707,7 +714,7 @@
             copy.start()
     for copy in passing:
         copy.start()
-    outs = []
+    outs = [pltpu.make_async_copy(v, b, pass_sem.at[1, i]) for i, (_, v, b) in enumerate(through)]
     for i in range(steps):
         unit, k = divmod(i, TAPS + 1)
         for copy in ins[i]:
@@ -721,7 +728,11 @@
                  pltpu.make_async_copy(wide_w.at[i], to, out_sem.at[1, i])]
         outs[-2].start()
         outs[-1].start()
-    for copy in outs + passing:
+        if i == 2:
+            for copy, on in zip(passing, outs):
+                copy.wait()
+                on.start()
+    for copy in outs:
         copy.wait()
 
 
@@ -746,7 +757,10 @@
             pltpu.VMEM(fw.shape, BF16),
             pltpu.VMEM((steps, 2 * C, C), F32),
             pltpu.VMEM((steps, C, C), F32),
-            dma((2, steps)), dma((2, steps)), dma((3,)),
+            pltpu.VMEM(out.shape, out.dtype),
+            pltpu.VMEM(sg.shape, sg.dtype),
+            pltpu.VMEM(ga.shape, ga.dtype),
+            dma((2, steps)), dma((2, steps)), dma((2, 3)),
         ],
         compiler_params=pltpu.CompilerParams(vmem_limit_bytes=63 * 1024 * 1024),
         name="widen",

time: 163 us -> 115 us (0.71)
  Pallas kernels: 163 us -> 114 us
    pallas_call x1, Pallas kernels: 41.7 us -> 8.78 us  [widen(): pl.pallas_call(widen_kernel, out_shape=(jax.ShapeDtypeStruct((steps, 2 *...]
    pallas_call x1, Pallas kernels: 121 us -> 105 us  [block_and_sums(): pl.pallas_call(functools.partial(block_kernel, samples), out_shape=outs,...]
where the time goes in v1:
time: 115 us
  Pallas kernels  114 us (99%)
    pallas_call x1, Pallas kernels, block_and_sums(): pl.pallas_call(functools.partial(block_kernel, samples), out_shape=outs,...  105 us
    pallas_call x1, Pallas kernels, widen(): pl.pallas_call(widen_kernel, out_shape=(jax.ShapeDtypeStruct((steps, 2 *...  8.78 us

profile of v1, /device:TPU:1, one launch (start us, length us, event | category | flops | bytes accessed | tf_op | source)
XLA Modules:
  0.0 114.7 jit_solution(4247000444442865419)
XLA Ops:
  0.6 105.1 %encoder_block.1 = (bf16[512,256]{1,0:T(8,128)(2,1)}, bf16[256,2048]{1,0:T(8,128)(2,1)}, bf16[16384,128]{1,0:T(8,128)(2,1)}, bf16[8192,128]{1,0:T(8,128)(2,1)}, f32[8,256]{1,0:T(8,128)}) custom-call(s32[1,5]{1,0:T(1,128)} %len_ref.1, bf16[256,2048]{1,0:T(8,128)(2,1)} %bitcast.5, bf16[512,256]{1,0:T(8,128)(2,1)} %bitcast.6, bf16[2,256,1792]{2,1,0:T(8,128)(2,1)} %wd_ref.1, ...), custom_call_target="tpu_custom_call" | custom-call | tf_op jit(solution)/shard_map/encoder_block/pallas_call | solution.py:690
  105.7 8.8 %widen.1 = (f32[16,512,256]{2,1,0:T(8,128)}, f32[2,256,1792]{2,1,0:T(8,128)}, f32[2,256,256]{2,1,0:T(8,128)}, bf16[512,256]{1,0:T(8,128)(2,1)}, bf16[256,2048]{1,0:T(8,128)(2,1)}, /*index=5*/f32[8,256]{1,0:T(8,128)}) custom-call(bf16[16384,128]{1,0:T(8,128)(2,1)} %get-tuple-element.17.dn_ref, bf16[8192,128]{1,0:T(8,128)(2,1)} %get-tuple-element.18.w_ref, ...), custom_call_target="tpu_custom_call" | custom-call | tf_op jit(solution)/shard_map/widen/pallas_call | solution.py:743

commit v2 on v1

--- a/solution.py
+++ b/solution.py
@@ -47,7 +47,7 @@
 MESH = pl.DeviceIdType.MESH
 ORDERS = ((0, 1, 2), (1, 2, 0), (2, 0, 1), (1, 2, 0), (2, 0, 1), (0, 1, 2), (2, 1, 0))
 N_DOWN = 3
-UNIT_OF = (0, 0, 1, 1)
+PLANE_JOBS = (3, 4)
 JOB_ROWS = (3072, 3072, 2048) + (1024,) * 4
 
 
@@ -59,11 +59,14 @@
         self.sibling = (self.dp + 1 - 2 * self.core, self.tm)
         self.sends = []
 
-    def along(self, axis, step):
+    def shifted(self, steps):
         x, y, z = (
-            lax.rem(c + step + RING, RING) if a == axis else c for a, c in enumerate(self.place)
+            lax.rem(c + steps[a] + RING, RING) if a in steps else c for a, c in enumerate(self.place)
         )
         return (y * 2 + self.core, z * RING + x)
+
+    def along(self, axis, step):
+        return self.shifted({axis: step})
 
     def in_time(self, step):
         count = lax.axis_size("tm")
@@ -71,7 +74,9 @@
 
     def peers(self):
         ring = [self.along(a, s) for a in range(3) for s in (1, 2, 3)]
-        return [self.sibling, self.in_time(1), self.in_time(-1)] + ring
+        planes = [ORDERS[p][1:] for p in PLANE_JOBS]
+        rest = [self.shifted({a: i, b: j}) for a, b in planes for i in (1, 2, 3) for j in (1, 2, 3)]
+        return [self.sibling, self.in_time(1), self.in_time(-1)] + ring + rest
 
     def greet(self):
         barrier = pltpu.get_barrier_semaphore()
@@ -102,7 +107,7 @@
                  cols, af0, af1, df0, df1, u0, u1, a0, b0, b1, grad, slope, sa, tr, zcols,
                  gb, gtf, gt, wt, wpt, rem, kcol, acc, hbuf, wdn_ref, gdn, gw, ga,
                  pr, lands, fin, gr, gat,
-                 load_sem, halo_s, halo_r, pair_s, pair_r, rs_s, rs_r, ag_s, ag_r, fin_sem, back_s, back_r, ga_s, ga_r):
+                 load_sem, halo_s, halo_r, pair_s, pair_r, rs_s, rs_r, ag_s, ag_r, rsp_s, rsp_r, agp_s, agp_r, fin_sem, back_s, back_r, ga_s, ga_r):
     load = pltpu.make_async_copy(wdn_hbm, wdn_ref, load_sem)
     load.start()
     links = Links()
@@ -112,9 +117,10 @@
     def start(job):
         next(job)
         jobs.append(job)
-
-    def tick():
-        for job in list(jobs):
+        return job
+
+    def tick(which=None):
+        for job in list(jobs if which is None else which):
             if next(job, True):
                 jobs.remove(job)
 
@@ -135,11 +141,8 @@
 
     def job_rows(p, hf):
         if p < N_DOWN:
-            return gdn, fdn_ref, hf * sum(JOB_ROWS[:N_DOWN]) + sum(JOB_ROWS[:p])
-        unit = UNIT_OF[p - N_DOWN]
-        before = sum(JOB_ROWS[q] for q in range(N_DOWN, p) if UNIT_OF[q - N_DOWN] == unit)
-        half = sum(JOB_ROWS[q] for q in range(N_DOWN, len(ORDERS)) if UNIT_OF[q - N_DOWN] == unit)
-        return gw, fw_ref, unit * 2 * half + hf * half + before
+            return gdn, fdn_ref, 2 * sum(JOB_ROWS[:p]) + hf * JOB_ROWS[p]
+        return gw, fw_ref, 2 * sum(JOB_ROWS[N_DOWN:p]) + hf * JOB_ROWS[p]
 
     def at(ref, start, count):
         return ref.at[pl.ds(pl.multiple_of(start, 16), count), :]
@@ -185,7 +188,24 @@
         links.remote(w, w, pair_s.at[p], pair_r.at[p], links.sibling).wait_recv()
         add_rows(w, 0, ((w, 0), (src, own_row)), part)
         base, bases, free = 0, [], 0
-        for s in range(3):
+        direct = p in PLANE_JOBS
+        plane = axes[1:]
+        small = chunk // RING**2
+        offsets = [(i, j) for i in range(RING) for j in range(RING) if i or j]
+        offsets.sort(key=lambda o: -(min(o[0], RING - o[0]) + min(o[1], RING - o[1])))
+        slots = {o: i for i, o in enumerate(offsets)}
+
+        def in_plane(step):
+            return links.shifted(dict(zip(plane, step)))
+
+        def plane_sems(step, sems):
+            i = PLANE_JOBS.index(p) * 15 + slots[step]
+            return sems[0].at[i], sems[1].at[i]
+
+        def small_row(step):
+            return base + (wrap(place[plane[0]] + step[0]) * RING + wrap(place[plane[1]] + step[1])) * small
+
+        for s in range(1 if direct else 3):
             q = part // RING ** (s + 1)
             h = q // 2
             me = place[axes[s]]
@@ -218,15 +238,34 @@
                     whole = land.at[free + (k - 1) * q : free + k * q, :]
                     links.remote(whole, whole, *rs(s, k), links.along(axes[s], k)).wait_recv()
                 terms = ((w, here),) + tuple((land, free + i * q) for i in range(3))
-            if s < 2:
+            if s < 2 or direct:
                 add_rows(w, here, terms, q)
             else:
                 add_rows(last, 0, terms, q)
             base = here
             free += 3 * q
-        keep_fin = pltpu.make_async_copy(last, result(base, q), fin_sem.at[p])
+        if direct:
+            q = small
+            mine = small_row((0, 0))
+            for step in offsets:
+                links.send(at(w, small_row(step), small), land.at[free + slots[step] * small : free + (slots[step] + 1) * small, :],
+                           *plane_sems(step, (rsp_s, rsp_r)), in_plane(step))
+            yield False
+            for step in offsets[::-1]:
+                block = land.at[free + slots[step] * small : free + (slots[step] + 1) * small, :]
+                links.remote(block, block, *plane_sems(step, (rsp_s, rsp_r)), in_plane(step)).wait_recv()
+            add_rows(last, 0, ((w, mine),) + tuple((land, free + i * small) for i in range(15)), small)
+        keep_fin = pltpu.make_async_copy(last, result(mine if direct else base, q), fin_sem.at[p])
         keep_fin.start()
-        for s in (2, 1, 0):
+        if direct:
+            for step in offsets:
+                links.send(last, result(mine, small), *plane_sems(step, (agp_s, agp_r)), in_plane(step))
+            yield False
+            for step in offsets[::-1]:
+                block = result(small_row((-step[0], -step[1])), small)
+                links.remote(block, block, *plane_sems(step, (agp_s, agp_r)), in_plane(step)).wait_recv()
+            keep_fin.wait()
+        for s in (0,) if direct else (2, 1, 0):
             q = part // RING ** (s + 1)
             h = q // 2
             me = place[axes[s]]
@@ -297,20 +336,24 @@
         ends.append(total * TILE)
 
     def rem_body(i, _):
-        rows = pl.ds(pl.multiple_of(i * 32, 32), 32)
-        p = lax.broadcasted_iota(jnp.int32, (32, 128), 0) + (i * 32 - LEAD + anchor)
-        hi, lo = jnp.zeros_like(p), jnp.full_like(p, -1)
-        start = 0
-        for end in ends:
-            inside = (p >= start) & (p < end)
-            hi = jnp.where(inside, end - p, hi)
-            lo = jnp.where(inside, p - start, lo)
-            start = end
-        rem[0, rows, :] = hi
-        rem[1, rows, :] = lo
+        for n in range(7):
+            first = (i * 7 + n) * 32 - 96 + anchor
+            lo_end, hi_end = first + 32, first
+            start = 0
+            for end in ends:
+                inside = (first >= start) & (first < end)
+                lo_end = jnp.where(inside, start, lo_end)
+                hi_end = jnp.where(inside, end, hi_end)
+                start = end
+            p = lax.broadcasted_iota(jnp.int32, (32, 128), 0) + first
+            rows = pl.ds(pl.multiple_of((i * 7 + n) * 32 + 16, 16), 32)
+            rem[0, rows, :] = hi_end - p
+            rem[1, rows, :] = p - lo_end
         return 0
 
-    lax.fori_loop(0, rows_all // 32, rem_body, 0)
+    rem[:, 0:16, :] = jnp.full((2, 16, 128), -1, jnp.int32)
+    rem[:, rows_all - 16 : rows_all, :] = jnp.full((2, 16, 128), -1, jnp.int32)
+    lax.fori_loop(0, (rows_all - 32) // (7 * 32), rem_body, 0)
 
     for i in range(5):
         row = jnp.broadcast_to(al_ref[i : i + 1, :], (8, C))
@@ -358,7 +401,7 @@
 
             lax.fori_loop(0, (b - a) // (32 * many), step, 0)
 
-    def pipelined(span, blocks, product, use):
+    def pipelined(span, blocks, product, use, mid=None):
         lo, hi = span
         count = (hi - lo) // 32
         starts = [lo + 32 * (count * n // blocks) for n in range(blocks + 1)]
@@ -373,6 +416,8 @@
             if n + 1 < blocks:
                 make(n + 1)
             use(pieces(a, b), hbuf.at[n % 2])
+            if n == 1 and mid is not None:
+                mid()
 
     def forward_weights(unit):
         for k in range(TAPS):
@@ -489,6 +534,13 @@
             elif by >= STRIDE:
                 z = jnp.where(after > by, z, 0.0)
             zcols[k, :, halves[h]] = z.astype(BF16)
+        d = dot(og_ref[...], zcols[k]).astype(BF16)
+        for h in range(2):
+            gdn[(2 * k + h) * 2 * C : (2 * k + h + 1) * 2 * C, :] = d[:, halves[h]]
+        for p in range(N_DOWN):
+            if 2 * sum(JOB_ROWS[: p + 1]) == (k + 1) * 4 * C:
+                start(job(p))
+
 
     gtf[8 : 8 + rows_j + 32, :] = gb[...].astype(F32)
     at_m = pl.ds(wide[0], all_j, stride=STRIDE)
@@ -500,26 +552,6 @@
         gt[2, :, lanes] = jnp.where(after > STRIDE, gtf[17 : 17 + all_j, lanes], 0.0).astype(BF16)
 
     load.wait()
-
-    own = og_ref[...]
-
-    def down_body(k, _):
-        d = dot(own, zcols[k]).astype(BF16)
-        for h in range(2):
-            gdn[pl.ds(pl.multiple_of((2 * k + h) * 2 * C, 16), 2 * C), :] = d[:, halves[h]]
-        return 0
-
-    lax.fori_loop(0, 2 * STRIDE, down_body, 0)
-    for p in range(N_DOWN):
-        start(job(p))
-
-    for o in range(2):
-        rows = slice(o * C, (o + 1) * C)
-        total = dot_nt(wdn_ref[0, rows, :], zcols[0])
-        for k in range(1, 2 * STRIDE):
-            total = total + dot_nt(wdn_ref[k, rows, :], zcols[k])
-        out_ref[rows, :] = total.astype(BF16)
-
     for p in range(STRIDE):
         if p < STRIDE // 2:
             d = dot(gt[1], wdn_ref[p + 12])
@@ -585,13 +617,14 @@
         tick()
         lax.fori_loop(0, samples // 512, transposed_e, 0)
 
+        started = []
         for k in range(TAPS):
             put_gw(unit, k, dot(tr[...], cols[own0:own1, k * C : (k + 1) * C]))
-        for p, of in enumerate(UNIT_OF):
-            if of == unit:
-                start(job(N_DOWN + p))
+            if k == TAPS // 2:
+                started.append(start(job(N_DOWN + 2 * unit)))
         if unit == 0:
-            tick()
+            tick([j for j in jobs if j not in started])
+        started.append(start(job(N_DOWN + 2 * unit + 1)))
 
         span = (own_rows, near)[unit]
         for k in range(TAPS):
@@ -611,7 +644,7 @@
                         sums.add(h, f * sa[ui, r, halves[h]].astype(F32))
             sums.store()
 
-        pipelined(span, 4, lambda rows: dot(cols[rows, :], wt[...]), inner)
+        pipelined(span, 4, lambda rows: dot(cols[rows, :], wt[...]), inner, lambda: tick(started) if unit == 0 else None)
         tick()
 
     backward(1)
@@ -622,6 +655,13 @@
         for h in range(2):
             ga[i : i + 1, halves[h]] = jnp.sum(acc[i, h] * kcol[1, i, h], axis=0, keepdims=True)
     start(alpha_job())
+
+    for o in range(2):
+        rows = slice(o * C, (o + 1) * C)
+        total = dot_nt(wdn_ref[0, rows, :], zcols[0])
+        for k in range(1, 2 * STRIDE):
+            total = total + dot_nt(wdn_ref[k, rows, :], zcols[k])
+        out_ref[rows, :] = total.astype(BF16)
 
     def sg_body(j, _):
         lanes = pl.ds(pl.multiple_of(j * 512, 128), 512)
@@ -685,6 +725,7 @@
         pltpu.VMEM((4, 8, C), F32),
         dma, dma((4,)), dma((4,)), dma((n_jobs,)), dma((n_jobs,)),
         dma((12 * n_jobs,)), dma((12 * n_jobs,)), dma((12 * n_jobs,)), dma((12 * n_jobs,)),
+        dma((30,)), dma((30,)), dma((30,)), dma((30,)),
         dma((n_jobs,)), dma((n_jobs, 4)), dma((n_jobs, 4)), dma((4, RING)), dma((4, RING)),
     ]
     return pl.pallas_call(

time: 115 us -> 105 us (0.913)
  Pallas kernels: 114 us -> 103 us
    pallas_call x1, Pallas kernels: 105 us -> 94.7 us  [block_and_sums(): pl.pallas_call(functools.partial(block_kernel, samples), out_shape=outs,...]
where the time goes in v2:
time: 105 us; the launch traced here: 104 us
  Pallas kernels  103 us (98%)
    pallas_call x1, Pallas kernels, block_and_sums(): pl.pallas_call(functools.partial(block_kernel, samples), out_shape=outs,...  94.7 us
    pallas_call x1, Pallas kernels, widen(): pl.pallas_call(widen_kernel, out_shape=(jax.ShapeDtypeStruct((steps, 2 *...  8.78 us

profile of v2, /device:TPU:1, one launch (start us, length us, event | category | flops | bytes accessed | tf_op | source)
XLA Modules:
  0.0 104.3 jit_solution(11566437838069271119)
XLA Ops:
  0.6 94.7 %encoder_block.1 = (bf16[512,256]{1,0:T(8,128)(2,1)}, bf16[256,2048]{1,0:T(8,128)(2,1)}, bf16[16384,128]{1,0:T(8,128)(2,1)}, bf16[8192,128]{1,0:T(8,128)(2,1)}, f32[8,256]{1,0:T(8,128)}) custom-call(s32[1,5]{1,0:T(1,128)} %len_ref.1, bf16[256,2048]{1,0:T(8,128)(2,1)} %bitcast.5, bf16[512,256]{1,0:T(8,128)(2,1)} %bitcast.6, bf16[2,256,1792]{2,1,0:T(8,128)(2,1)} %wd_ref.1, ...), custom_call_target="tpu_custom_call" | custom-call | tf_op jit(solution)/shard_map/encoder_block/pallas_call | solution.py:731
  95.3 8.8 %widen.1 = (f32[16,512,256]{2,1,0:T(8,128)}, f32[2,256,1792]{2,1,0:T(8,128)}, f32[2,256,256]{2,1,0:T(8,128)}, bf16[512,256]{1,0:T(8,128)(2,1)}, bf16[256,2048]{1,0:T(8,128)(2,1)}, /*index=5*/f32[8,256]{1,0:T(8,128)}) custom-call(bf16[16384,128]{1,0:T(8,128)(2,1)} %get-tuple-element.17.dn_ref, bf16[8192,128]{1,0:T(8,128)(2,1)} %get-tuple-element.18.w_ref, ...), custom_call_target="tpu_custom_call" | custom-call | tf_op jit(solution)/shard_map/widen/pallas_call | solution.py:784
